TPU v7x, 32 devices: a whole 2x2x4 slice. The times are simulated.
32 devices in a mesh: dp: 4 (over x, core), expert: 8 (over z, y).
Axes of the slice: x: 2, y: 2, z: 4, core: 2. Of those that a mesh axis runs over, the one named last changes fastest.
Arguments:
- tokens: bfloat16 [128, 7168], P(('dp', 'expert')), may hold values from -6 to 6
- routes: int32 [128, 8], P(('dp', 'expert')), may hold values from 0 to 31, all different within a row; in each aligned block of 4 rows (0 to 3, 4 to 7, ...) at most 2 rows name the same one
- gate_scores: float32 [128, 8], P(('dp', 'expert')), may hold values from 0.1 to 1
- w_gate: bfloat16 [32, 7168, 2048], P('expert', None, 'dp'), may hold values from -0.0625 to 0.0625
- w_up: bfloat16 [32, 7168, 2048], P('expert', None, 'dp'), may hold values from -0.0625 to 0.0625
- w_down: bfloat16 [32, 2048, 7168], P('expert', None, 'dp'), may hold values from -0.125 to 0.125
Outputs:
- combined: bfloat16 [128, 7168], P(('dp', 'expert'))
Inputs may be any that keep to these rules, and one draw needn't show every extreme that they name: `routes`: each row names 8 different experts; among the rows of one device no expert is named more than 2 times, a bound that some block reaches.
All inputs are finite; a program needn't handle non-finite values.
Results may differ from a plain program's by a relative error of at most 0.0057.
Values may be sent and summed in bfloat16 or wider, within the bound.
A program may use at most 192 MiB of HBM per device.

v0:
```python
import jax
import jax.numpy as jnp
from jax import lax
from jax.sharding import PartitionSpec as P

D = 7168
TOPK = 8
E = 32
CAP = 2


def slot_codes(route_block):
    route_list = route_block.reshape(-1)
    onehot = (route_list[:, None] == jnp.arange(E, dtype=jnp.int32)[None, :]).astype(jnp.int32)
    before = jnp.cumsum(onehot, axis=0) - onehot
    return (route_list * CAP + jnp.sum(before * onehot, axis=1)).reshape(route_block.shape)


def selection(route_block):
    codes = slot_codes(route_block)
    hits = codes[None, :, :] == jnp.arange(E * CAP, dtype=jnp.int32)[:, None, None]
    return jnp.any(hits, axis=2).astype(jnp.bfloat16)


def expert_hidden(rows_in, gate_local, up_local):
    gate_part = jnp.einsum("erk,ekf->erf", rows_in, gate_local, preferred_element_type=jnp.float32)
    up_part = jnp.einsum("erk,ekf->erf", rows_in, up_local, preferred_element_type=jnp.float32)
    return (jax.nn.silu(gate_part) * up_part).astype(jnp.bfloat16)


def body(tokens, routes, gate_scores, w_gate, w_up, w_down):
    n_data = lax.axis_size("dp")
    n_group = lax.axis_size("expert")
    local_experts = w_gate.shape[0]
    tok_count = tokens.shape[0]
    all_tokens, all_routes = (
        lax.all_gather(tokens, "dp", axis=0, tiled=True),
        lax.all_gather(routes, "dp", axis=0, tiled=True),
    )
    route_blocks = all_routes.reshape(n_data, tok_count, TOPK)
    chosen = jax.vmap(selection)(route_blocks).reshape(n_data, E, CAP, tok_count)
    token_blocks = all_tokens.reshape(n_data, tok_count, D)
    outgoing = jnp.einsum(
        "decn,dnk->edck", chosen, token_blocks, preferred_element_type=jnp.float32
    ).astype(jnp.bfloat16)
    arrived = lax.all_to_all(outgoing, "expert", split_axis=0, concat_axis=2, tiled=True)
    items = arrived.shape[1]
    merged = arrived.reshape(local_experts, items * arrived.shape[2], D)
    result = expert_hidden(merged, w_gate, w_up)
    hidden_split = result.reshape(local_experts, items, arrived.shape[2], w_gate.shape[2])
    hidden = hidden_split.reshape(local_experts, n_data * n_group * CAP, w_gate.shape[2])
    width_local = w_down.shape[2]
    expert_out = jnp.einsum(
        "erf,efk->erk",
        lax.all_gather(hidden, "dp", axis=2, tiled=True),
        w_down,
        preferred_element_type=jnp.float32,
    ).astype(jnp.bfloat16)
    expert_out = expert_out.reshape(local_experts, n_data, n_group, CAP, width_local)
    returned = lax.all_to_all(
        lax.all_to_all(expert_out, "dp", split_axis=1, concat_axis=4, tiled=True),
        "expert",
        split_axis=2,
        concat_axis=0,
        tiled=True,
    )
    returned = returned.reshape(E * CAP, D)
    codes = slot_codes(routes)
    matches = codes[:, :, None] == jnp.arange(E * CAP, dtype=jnp.int32)[None, None, :]
    weighting = jnp.sum(jnp.where(matches, gate_scores[:, :, None], 0.0), axis=1)
    combined = jnp.dot(weighting, returned.astype(jnp.float32), precision=lax.Precision.HIGHEST)
    return combined.astype(jnp.bfloat16)


def solution(mesh):
    placed = (
        P(("dp", "expert"), None),
        P(("dp", "expert"), None),
        P(("dp", "expert"), None),
        P("expert", None, "dp"),
        P("expert", None, "dp"),
        P("expert", None, "dp"),
    )
    return jax.shard_map(
        body, mesh=mesh, in_specs=placed, out_specs=P(("dp", "expert"), None), check_vma=False
    )
```

profile of v0, /device:TPU:0, one launch (start us, length us, event | category | flops | bytes accessed | tf_op | source)
XLA Modules:
  0.0 237.9 jit_solution(15998013190049495341)
XLA Ops:
  6.5 0.0 all-gather.4.cloned.1.call-start
  6.5 6.3 %all-gather = s32[4,4,8]{2,1,0:T(4,128)S(1)} all-gather(s32[1,4,8]{2,1,0:T(4,128)} %bitcast.38), channel_id=1, replica_groups=mesh['dp'=4,'expert'=8] {'dp'}, dimensions={0}, use_global_device_ids=true | all-gather | bytes 640 | tf_op jit(solution)/shard_map/all_gather | solution.py:38
  12.8 0.1 eq.63
  12.9 0.1 fusion.4
  13.0 0.1 reduce_window_sum.23
  13.0 0.2 select_reduce_fusion
  13.3 0.1 reduce_sum.35
  13.4 0.1 fusion.5
  13.5 0.1 copy.18
  13.6 6.3 %all-gather.1 = bf16[4,4,7168]{2,1,0:T(4,128)(2,1)S(1)} all-gather(bf16[1,4,7168]{2,1,0:T(4,128)(2,1)} %bitcast.37), channel_id=1, replica_groups=mesh['dp'=4,'expert'=8] {'dp'}, dimensions={0}, use_global_device_ids=true | all-gather | bytes 286720 | tf_op jit(solution)/shard_map/all_gather | solution.py:37
  19.9 1.1 fusion
  21.0 3.8 %copy.20 = bf16[32,4,2,7168]{3,2,1,0:T(2,128)(2,1)S(1)} copy(bf16[32,4,2,7168]{3,0,2,1:T(8,128)(2,1)S(1)} %fusion) | data formatting | bytes 7340032 | tf_op jit(solution)/shard_map/convert_element_type | solution.py:45
  24.8 88.2 %all_to_all.48 = bf16[32,4,2,7168]{3,2,1,0:T(2,128)(2,1)S(1)} all-to-all(bf16[32,4,2,7168]{3,2,1,0:T(2,128)(2,1)S(1)} %copy.20), channel_id=1, replica_groups=mesh['dp'=4,'expert'=8] {'expert'}, dimensions={0} | all-to-all | bytes 7340032 | tf_op jit(solution)/shard_map/all_to_all | solution.py:46
  112.9 5.5 %copy.31 = bf16[8,4,4,2,7168]{4,3,0,2,1:T(2,128)(2,1)} copy(bf16[8,4,4,2,7168]{4,3,2,1,0:T(2,128)(2,1)S(1)} %bitcast.32) | data formatting | bytes 7340032 | tf_op jit(solution)/shard_map/all_to_all | solution.py:46
  118.4 8.4 %reshape.42 = bf16[4,64,7168]{2,1,0:T(8,128)(2,1)} reshape(bf16[4,4,8,2,7168]{4,3,2,1,0:T(2,128)(2,1)} %bitcast.33) | data formatting | bytes 7340032 | tf_op jit(solution)/shard_map/reshape | solution.py:48
  126.8 0.0 copy-start
  126.8 13.1 %fusion.7 = f32[4,64,512]{2,1,0:T(8,128)S(1)} fusion(bf16[4,64,7168]{2,1,0:T(8,128)(2,1)} %reshape.42, bf16[4,7168,512]{2,1,0:T(8,128)(2,1)} %param.9), kind=kOutput, calls=%fused_computation.21 | convolution fusion | flops 1879048192 | bytes 33554432 | tf_op jit(solution)/shard_map/erk,ekf->erf/dot_general | solution.py:26
  139.9 0.0 copy-done
  139.9 12.9 %fusion.1 = bf16[4,64,512]{2,1,0:T(8,128)(2,1)} fusion(bf16[4,64,7168]{2,1,0:T(8,128)(2,1)S(1)} %copy-done, bf16[4,7168,512]{2,1,0:T(8,128)(2,1)} %param.10, f32[4,64,512]{2,1,0:T(8,128)S(1)} %fusion.7), kind=kOutput, calls=%fused_computation.6 | convolution fusion | flops 1879834624 | bytes 33816576 | tf_op jit(solution)/shard_map/erk,ekf->erf/dot_general | solution.py:27
  152.8 0.0 all-gather.4.cloned.1.call-update
  152.8 15.9 %all-gather.4.cloned.1.call-done = bf16[4,64,2048]{2,1,0:T(8,128)(2,1)} async-done(((bf16[4,64,512]{2,1,0:T(8,128)(2,1)}), bf16[4,64,2048]{2,1,0:T(8,128)(2,1)}) %all-gather.4.cloned.1.call-update) | async-done | bytes 1048592 | tf_op jit(solution)/shard_map/all_gather | solution.py:55
  168.8 14.6 %convolution_convert_fusion.2 = bf16[4,64,1792]{2,1,0:T(8,128)(2,1)S(1)} fusion(bf16[4,64,2048]{2,1,0:T(8,128)(2,1)} %all-gather.4.cloned.1.call-done, bf16[4,2048,1792]{2,1,0:T(8,128)(2,1)} %param.11), kind=kOutput, calls=%fused_computation.4 | convolution fusion | flops 1879506944 | bytes 31326208 | tf_op jit(solution)/shard_map/erf,efk->erk/dot_general | solution.py:53
  183.4 0.0 copy-start.1
  183.4 0.0 copy-start.2
  183.4 0.3 reshape.43
  183.8 0.1 copy.22
  183.9 15.5 %all_to_all.49 = bf16[4,4,8,2,1792]{4,2,3,0,1:T(8,128)(2,1)S(1)} all-to-all(bf16[4,4,8,2,1792]{4,2,3,0,1:T(8,128)(2,1)S(1)} %copy.22), channel_id=1, replica_groups=mesh['dp'=4,'expert'=8] {'dp'}, dimensions={1} | all-to-all | bytes 1835008 | tf_op jit(solution)/shard_map/all_to_all | solution.py:61
  199.3 0.7 copy.26
  200.1 1.3 reshape.55
  201.3 5.5 %all-to-all-start.2 = ((bf16[4,1,8,2,7168]{4,3,0,1,2:T(2,128)(2,1)}), bf16[4,1,8,2,7168]{4,3,0,1,2:T(2,128)(2,1)S(1)}, u32[]{:S(2)}, u32[]{:S(2)}) async-start(bf16[4,1,8,2,7168]{4,3,0,1,2:T(2,128)(2,1)} %reshape.55), calls=%async_computation.2 | async-start | bytes 1835008 | tf_op jit(solution)/shard_map/all_to_all | solution.py:60
  206.8 0.0 copy-done.1
  206.8 0.1 eq.56
  206.9 0.1 fusion.6
  207.0 0.1 reduce_window_sum.22
  207.1 0.2 select_reduce_fusion.2
  207.2 0.1 reduce_sum.32
  207.3 0.0 copy-done.2
  207.3 0.1 select_reduce_fusion.1
  207.4 22.2 %all-to-all-done.2 = bf16[4,1,8,2,7168]{4,3,0,1,2:T(2,128)(2,1)S(1)} async-done(((bf16[4,1,8,2,7168]{4,3,0,1,2:T(2,128)(2,1)}), bf16[4,1,8,2,7168]{4,3,0,1,2:T(2,128)(2,1)S(1)}, u32[]{:S(2)}, u32[]{:S(2)}) %all-to-all-start.2) | async-done | bytes 917536 | tf_op jit(solution)/shard_map/all_to_all | solution.py:60
  229.7 0.3 reshape.44
  230.0 1.1 convolution_convert_fusion.1
  (2 shorter events, 0.0 us)
Async XLA Ops:
  6.5 162.2 %all-gather.4.cloned.1.call-start = ((), (), s32[]{:S(2)}) async-start(), calls=%async_computation.3 | async-start | bytes 1310720 | tf_op jit(solution)/shard_map/all_gather | solution.py:55
  126.8 13.1 %copy-start = (bf16[4,64,7168]{2,1,0:T(8,128)(2,1)S(1)}, bf16[4,64,7168]{2,1,0:T(8,128)(2,1)}, u32[]{:S(2)}) copy-start(bf16[4,64,7168]{2,1,0:T(8,128)(2,1)} %reshape.42) | copy-start | bytes 11010052
  183.4 23.5 %copy-start.1 = (s32[4,8]{1,0:T(4,128)S(1)}, s32[4,8]{1,0:T(4,128)}, u32[]{:S(2)}) copy-start(s32[4,8]{1,0:T(4,128)} %param.7) | copy-start | bytes 388
  183.4 23.9 %copy-start.2 = (f32[4,8]{1,0:T(4,128)S(1)}, f32[4,8]{1,0:T(4,128)}, u32[]{:S(2)}) copy-start(f32[4,8]{1,0:T(4,128)} %param.8) | copy-start | bytes 388
  201.3 28.3 %all-to-all-start.2 = ((bf16[4,1,8,2,7168]{4,3,0,1,2:T(2,128)(2,1)}), bf16[4,1,8,2,7168]{4,3,0,1,2:T(2,128)(2,1)S(1)}, u32[]{:S(2)}, u32[]{:S(2)}) async-start(bf16[4,1,8,2,7168]{4,3,0,1,2:T(2,128)(2,1)} %reshape.55), calls=%async_computation.2 | async-start | bytes 1835008 | tf_op jit(solution)/shard_map/all_to_all | solution.py:60
Sparse Core Ops, SparseCore 0:
  152.9 15.7 all-gather.3
where the time goes:
time: 238 us
  blocking collectives  116 us (49%)
  matrix products  42.8 us (18%)
  waiting for transfers between devices  38.2 us (16%)
  local copies, waits for them, and re-layouts  20.9 us (9%)
  between operations  13.5 us (6%)
  starting transfers between devices  5.52 us (2%)
    all_to_all x1, blocking collectives, body(): lax.all_to_all(outgoing, 'expert', split_axis=0, concat_axis=2, tiled=True)  88.2 us
    all_to_all x1, waiting for transfers between devices, body(): lax.all_to_all(lax.all_to_all(expert_out, 'dp', split_axis=1, concat_axis...  22.2 us
    all_gather x1, waiting for transfers between devices, body(): lax.all_gather(hidden, 'dp', axis=2, tiled=True)  15.9 us
    all_to_all x1, blocking collectives, body(): lax.all_to_all(expert_out, 'dp', split_axis=1, concat_axis=4, tiled=True)  15.5 us
    dot_general x1, matrix products, body(): jnp.einsum('erf,efk->erk', lax.all_gather(hidden, 'dp', axis=2, tiled=Tru...  14.6 us
    dot_general x1, matrix products, expert_hidden(): jnp.einsum('erk,ekf->erf', rows_in, gate_local, preferred_element_type=jn...  13.1 us
    dot_general x1, matrix products, expert_hidden(): jnp.einsum('erk,ekf->erf', rows_in, up_local, preferred_element_type=jnp....  12.9 us
    reshape x1, local copies, waits for them, and re-layouts, body(): merged = arrived.reshape(local_experts, items * arrived.shape[2], D)  8.4 us
  transfers between devices with their start and end apart: 2, of which 2 were waited for; matrix products, arithmetic and copies ran while one was open for 0% of the time, Pallas kernels for 0%

commit v1 on v0

--- a/solution.py
+++ b/solution.py
@@ -7,6 +7,22 @@
 TOPK = 8
 E = 32
 CAP = 2
+
+
+def summed_both_ways(value, axis, dim, term):
+    peers, place, rows = (lax.axis_size(axis), lax.axis_index(axis), value.shape[dim])
+    right = [(i, (i + 1) % peers) for i in range(peers)]
+    left = [(i, (i - 1) % peers) for i in range(peers)]
+    middle = peers // 2
+    from_left = from_right = value
+    running = term(value, place * rows)
+    for turn in range(1, middle + 1):
+        from_left = lax.ppermute(from_left, axis, right)
+        if turn < peers - middle:
+            from_right = lax.ppermute(from_right, axis, left)
+            running = running + term(from_right, (place + turn) % peers * rows)
+        running = running + term(from_left, (place - turn) % peers * rows)
+    return running
 
 
 def slot_codes(route_block):
@@ -50,11 +66,16 @@
     hidden_split = result.reshape(local_experts, items, arrived.shape[2], w_gate.shape[2])
     hidden = hidden_split.reshape(local_experts, n_data * n_group * CAP, w_gate.shape[2])
     width_local = w_down.shape[2]
-    expert_out = jnp.einsum(
-        "erf,efk->erk",
-        lax.all_gather(hidden, "dp", axis=2, tiled=True),
-        w_down,
-        preferred_element_type=jnp.float32,
+    expert_out = summed_both_ways(
+        hidden,
+        "dp",
+        2,
+        lambda shard, offset: jnp.einsum(
+            "erf,efk->erk",
+            shard,
+            lax.dynamic_slice_in_dim(w_down, offset, shard.shape[2], axis=1),
+            preferred_element_type=jnp.float32,
+        ),
     ).astype(jnp.bfloat16)
     expert_out = expert_out.reshape(local_experts, n_data, n_group, CAP, width_local)
     returned = lax.all_to_all(

time: 238 us -> 218 us (0.916)
  blocking collectives: 116 us -> 29.1 us
  waiting for transfers between devices: 38.2 us -> 105 us
  between operations: 13.5 us -> 0.14 us
  starting transfers between devices: 5.52 us -> 11.6 us
  local copies, waits for them, and re-layouts: 20.9 us -> 24.7 us
  matrix products: 42.8 us -> 45.4 us
    all_to_all x1 -> x0, blocking collectives: 88.2 us -> none  [body(): lax.all_to_all(outgoing, 'expert', split_axis=0, concat_axis=2, tiled=True)]
    all_to_all x0 -> x1, waiting for transfers between devices: none -> 82.6 us  [body(): lax.all_to_all(outgoing, 'expert', split_axis=0, concat_axis=2, tiled=True)]
    all_gather x1 -> x0, waiting for transfers between devices: 15.9 us -> none  [body(): lax.all_gather(hidden, 'dp', axis=2, tiled=True)]
    all_to_all x0 -> x1, starting transfers between devices: none -> 5.96 us  [body(): lax.all_to_all(outgoing, 'expert', split_axis=0, concat_axis=2, tiled=True)]
    dot_general x1 -> x4, matrix products: 14.6 us -> 17.9 us  [body(): jnp.einsum('erf,efk->erk', shard, lax.dynamic_slice_in_dim(w_down, offset...]
  transfers between devices with their start and end apart: 2 -> 5, of which waited for: 2 -> 3; matrix products, arithmetic and copies ran while one was open for 0% -> 6% of each run, Pallas kernels for 0% -> 0%
where the time goes in v1:
time: 218 us; the launch traced here: 217 us
  waiting for transfers between devices  105 us (48%)
  matrix products  45.4 us (21%)
  blocking collectives  29.1 us (13%)
  local copies, waits for them, and re-layouts  24.7 us (11%)
  starting transfers between devices  11.6 us (5%)
    all_to_all x1, waiting for transfers between devices, body(): lax.all_to_all(outgoing, 'expert', split_axis=0, concat_axis=2, tiled=True)  82.6 us
    all_to_all x1, waiting for transfers between devices, body(): lax.all_to_all(lax.all_to_all(expert_out, 'dp', split_axis=1, concat_axis...  22.3 us
    dot_general x4, matrix products, body(): jnp.einsum('erf,efk->erk', shard, lax.dynamic_slice_in_dim(w_down, offset...  17.9 us
    all_to_all x1, blocking collectives, body(): lax.all_to_all(expert_out, 'dp', split_axis=1, concat_axis=4, tiled=True)  16.6 us
    dot_general x1, matrix products, expert_hidden(): jnp.einsum('erk,ekf->erf', rows_in, gate_local, preferred_element_type=jn...  13.1 us
    dot_general x1, matrix products, expert_hidden(): jnp.einsum('erk,ekf->erf', rows_in, up_local, preferred_element_type=jnp....  12.2 us
    reshape x1, local copies, waits for them, and re-layouts, body(): merged = arrived.reshape(local_experts, items * arrived.shape[2], D)  8.4 us
    all_to_all x1, local copies, waits for them, and re-layouts, body(): lax.all_to_all(outgoing, 'expert', split_axis=0, concat_axis=2, tiled=True)  7.41 us
  transfers between devices with their start and end apart: 5, of which 3 were waited for; matrix products, arithmetic and copies ran while one was open for 6% of the time, Pallas kernels for 0%

profile of v1, /device:TPU:0, one launch (start us, length us, event | category | flops | bytes accessed | tf_op | source)
XLA Modules:
  0.0 217.2 jit_solution(7696155670127710246)
XLA Ops:
  0.0 6.3 %all-gather = s32[4,4,8]{2,1,0:T(4,128)S(1)} all-gather(s32[1,4,8]{2,1,0:T(4,128)} %bitcast.39), channel_id=1, replica_groups=mesh['dp'=4,'expert'=8] {'dp'}, dimensions={0}, use_global_device_ids=true | all-gather | bytes 640 | tf_op jit(solution)/shard_map/all_gather | solution.py:54
  6.3 0.1 eq.67
  6.3 0.1 fusion.24
  6.4 0.1 reduce_window_sum.23
  6.5 0.2 select_reduce_fusion
  6.7 0.1 reduce_sum.35
  6.8 0.1 fusion.25
  6.9 0.1 copy.18
  7.1 6.3 %all-gather.1 = bf16[4,4,7168]{2,1,0:T(4,128)(2,1)S(1)} all-gather(bf16[1,4,7168]{2,1,0:T(4,128)(2,1)} %bitcast.38), channel_id=1, replica_groups=mesh['dp'=4,'expert'=8] {'dp'}, dimensions={0}, use_global_device_ids=true | all-gather | bytes 286720 | tf_op jit(solution)/shard_map/all_gather | solution.py:53
  13.4 1.1 fusion
  14.4 5.6 %copy.20 = bf16[32,4,2,7168]{3,2,1,0:T(2,128)(2,1)} copy(bf16[32,4,2,7168]{3,0,2,1:T(8,128)(2,1)S(1)} %fusion) | data formatting | bytes 7340032 | tf_op jit(solution)/shard_map/convert_element_type | solution.py:61
  20.0 6.0 %all-to-all-start = ((bf16[32,4,2,7168]{3,2,1,0:T(2,128)(2,1)}), bf16[32,4,2,7168]{3,2,1,0:T(2,128)(2,1)}, u32[]{:S(2)}, u32[]{:S(2)}) async-start(bf16[32,4,2,7168]{3,2,1,0:T(2,128)(2,1)} %copy.20), calls=%async_computation | async-start | bytes 7340032 | tf_op jit(solution)/shard_map/all_to_all | solution.py:62
  26.0 82.6 %all-to-all-done = bf16[32,4,2,7168]{3,2,1,0:T(2,128)(2,1)} async-done(((bf16[32,4,2,7168]{3,2,1,0:T(2,128)(2,1)}), bf16[32,4,2,7168]{3,2,1,0:T(2,128)(2,1)}, u32[]{:S(2)}, u32[]{:S(2)}) %all-to-all-start) | async-done | bytes 3670048 | tf_op jit(solution)/shard_map/all_to_all | solution.py:62
  108.6 7.4 %copy.31 = bf16[8,4,4,2,7168]{4,3,0,2,1:T(2,128)(2,1)} copy(bf16[8,4,4,2,7168]{4,3,2,1,0:T(2,128)(2,1)} %bitcast.6) | data formatting | bytes 7340032 | tf_op jit(solution)/shard_map/all_to_all | solution.py:62
  116.0 8.4 %reshape.42 = bf16[4,64,7168]{2,1,0:T(8,128)(2,1)} reshape(bf16[4,4,8,2,7168]{4,3,2,1,0:T(2,128)(2,1)} %bitcast.34) | data formatting | bytes 7340032 | tf_op jit(solution)/shard_map/reshape | solution.py:64
  124.4 0.0 copy-start
  124.4 13.1 %fusion.31 = f32[4,64,512]{2,1,0:T(8,128)S(1)} fusion(bf16[4,64,7168]{2,1,0:T(8,128)(2,1)} %reshape.42, bf16[4,7168,512]{2,1,0:T(8,128)(2,1)} %param.9), kind=kOutput, calls=%fused_computation.36 | convolution fusion | flops 1879048192 | bytes 33554432 | tf_op jit(solution)/shard_map/erk,ekf->erf/dot_general | solution.py:42
  137.5 0.0 copy-done
  137.5 12.2 %fusion.21 = bf16[4,64,512]{2,1,0:T(8,128)(2,1)S(1)} fusion(bf16[4,64,7168]{2,1,0:T(8,128)(2,1)S(1)} %copy-done, bf16[4,7168,512]{2,1,0:T(8,128)(2,1)} %param.10, f32[4,64,512]{2,1,0:T(8,128)S(1)} %fusion.31), kind=kOutput, calls=%fused_computation.17 | convolution fusion | flops 1879834624 | bytes 33816576 | tf_op jit(solution)/shard_map/erk,ekf->erf/dot_general | solution.py:43
  149.7 0.1 collective-permute-start.1
  149.7 1.7 collective-permute-start
  151.5 4.5 %fusion.7 = f32[4,64,1792]{2,1,0:T(8,128)S(1)} fusion(bf16[4,64,512]{2,1,0:T(8,128)(2,1)S(1)} %fusion.21, bf16[4,2048,1792]{2,1,0:T(8,128)(2,1)} %param.11, s32[]{:T(128)S(6)} %select_n.32), kind=kOutput, calls=%fused_computation.9 | convolution fusion | flops 469762048 | bytes 9437188 | tf_op jit(solution)/shard_map/erf,efk->erk/dot_general | solution.py:73
  155.9 0.5 collective-permute-done.1
  156.5 0.2 collective-permute-start.2
  156.7 4.5 %fusion.3 = f32[4,64,1792]{2,1,0:T(8,128)S(1)} fusion(bf16[4,64,512]{2,1,0:T(8,128)(2,1)S(1)} %collective-permute-done.1, bf16[4,2048,1792]{2,1,0:T(8,128)(2,1)} %param.11, s32[]{:T(128)S(6)} %select_n.36), kind=kOutput, calls=%fused_computation.5 | convolution fusion | flops 469762048 | bytes 9437188 | tf_op jit(solution)/shard_map/erf,efk->erk/dot_general | solution.py:73
  161.1 0.0 collective-permute-done
  161.1 4.5 %fusion.12 = f32[4,64,1792]{2,1,0:T(8,128)S(1)} fusion(f32[4,64,1792]{2,1,0:T(8,128)S(1)} %fusion.3, f32[4,64,1792]{2,1,0:T(8,128)S(1)} %fusion.7, bf16[4,64,512]{2,1,0:T(8,128)(2,1)S(1)} %collective-permute-done, bf16[4,2048,1792]{2,1,0:T(8,128)(2,1)} %param.11, s32[]{:T(128)S(6)} %select_n.34), kind=kOutput, calls=%fused_computation.13 | convolution fusion | flops 470679552 | bytes 13107204 | tf_op jit(solution)/shard_map/erf,efk->erk/dot_general | solution.py:73
  165.7 0.0 collective-permute-done.2
  165.7 4.5 %fusion.18 = bf16[4,64,1792]{2,1,0:T(8,128)(2,1)S(1)} fusion(f32[4,64,1792]{2,1,0:T(8,128)S(1)} %fusion.12, bf16[4,64,512]{2,1,0:T(8,128)(2,1)S(1)} %collective-permute-done.2, bf16[4,2048,1792]{2,1,0:T(8,128)(2,1)} %param.11, s32[]{:T(128)S(6)} %select_n.38), kind=kOutput, calls=%fused_computation.15 | convolution fusion | flops 470679552 | bytes 10354692 | tf_op jit(solution)/shard_map/erf,efk->erk/dot_general | solution.py:73
  170.1 0.0 copy-start.1
  170.2 0.0 copy-start.2
  170.2 0.3 reshape.43
  170.5 0.1 copy.22
  170.6 16.6 %all_to_all.48 = bf16[4,4,8,2,1792]{4,2,3,0,1:T(8,128)(2,1)S(1)} all-to-all(bf16[4,4,8,2,1792]{4,2,3,0,1:T(8,128)(2,1)S(1)} %copy.22), channel_id=1, replica_groups=mesh['dp'=4,'expert'=8] {'dp'}, dimensions={1} | all-to-all | bytes 1835008 | tf_op jit(solution)/shard_map/all_to_all | solution.py:82
  187.2 0.7 copy.26
  187.9 1.3 reshape.55
  189.2 3.6 %all-to-all-start.2 = ((bf16[4,1,8,2,7168]{4,3,0,1,2:T(2,128)(2,1)}), bf16[4,1,8,2,7168]{4,3,0,1,2:T(2,128)(2,1)S(1)}, u32[]{:S(2)}, u32[]{:S(2)}) async-start(bf16[4,1,8,2,7168]{4,3,0,1,2:T(2,128)(2,1)} %reshape.55), calls=%async_computation.2 | async-start | bytes 1835008 | tf_op jit(solution)/shard_map/all_to_all | solution.py:81
  192.8 0.0 copy-done.1
  192.9 0.1 eq.60
  192.9 0.1 fusion.26
  193.0 0.1 reduce_window_sum.22
  193.1 0.2 select_reduce_fusion.2
  193.2 0.1 reduce_sum.32
  193.3 0.0 copy-done.2
  193.3 0.1 select_reduce_fusion.1
  193.4 22.3 %all-to-all-done.2 = bf16[4,1,8,2,7168]{4,3,0,1,2:T(2,128)(2,1)S(1)} async-done(((bf16[4,1,8,2,7168]{4,3,0,1,2:T(2,128)(2,1)}), bf16[4,1,8,2,7168]{4,3,0,1,2:T(2,128)(2,1)S(1)}, u32[]{:S(2)}, u32[]{:S(2)}) %all-to-all-start.2) | async-done | bytes 917536 | tf_op jit(solution)/shard_map/all_to_all | solution.py:81
  215.7 0.3 reshape.44
  216.1 1.1 convolution_convert_fusion.1
  (2 shorter events, 0.0 us)
Async XLA Ops:
  20.0 88.5 %all-to-all-start = ((bf16[32,4,2,7168]{3,2,1,0:T(2,128)(2,1)}), bf16[32,4,2,7168]{3,2,1,0:T(2,128)(2,1)}, u32[]{:S(2)}, u32[]{:S(2)}) async-start(bf16[32,4,2,7168]{3,2,1,0:T(2,128)(2,1)} %copy.20), calls=%async_computation | async-start | bytes 7340032 | tf_op jit(solution)/shard_map/all_to_all | solution.py:62
  124.4 13.1 %copy-start = (bf16[4,64,7168]{2,1,0:T(8,128)(2,1)S(1)}, bf16[4,64,7168]{2,1,0:T(8,128)(2,1)}, u32[]{:S(2)}) copy-start(bf16[4,64,7168]{2,1,0:T(8,128)(2,1)} %reshape.42) | copy-start | bytes 11010052
  149.7 6.8 %collective-permute-start.1 = (bf16[4,64,512]{2,1,0:T(8,128)(2,1)S(1)}, bf16[4,64,512]{2,1,0:T(8,128)(2,1)S(1)}, u32[]{:S(2)}, u32[]{:S(2)}) collective-permute-start(bf16[4,64,512]{2,1,0:T(8,128)(2,1)S(1)} %fusion.21), channel_id=1, source_target_pairs={{0,8},{8,16},{16,24},{24,0},{1,9},{9,17},{17,25},{25,1},{2,10},{10... | collective-permute-start | bytes 786440 | tf_op jit(solution)/shard_map/ppermute | solution.py:20
  149.7 11.4 %collective-permute-start = (bf16[4,64,512]{2,1,0:T(8,128)(2,1)S(1)}, bf16[4,64,512]{2,1,0:T(8,128)(2,1)S(1)}, u32[]{:S(2)}, u32[]{:S(2)}) collective-permute-start(bf16[4,64,512]{2,1,0:T(8,128)(2,1)S(1)} %fusion.21), channel_id=1, source_target_pairs={{0,24},{8,0},{16,8},{24,16},{1,25},{9,1},{17,9},{25,17},{2,26},{10... | collective-permute-start | bytes 786440 | tf_op jit(solution)/shard_map/ppermute | solution.py:22
  156.5 9.2 %collective-permute-start.2 = (bf16[4,64,512]{2,1,0:T(8,128)(2,1)S(1)}, bf16[4,64,512]{2,1,0:T(8,128)(2,1)S(1)}, u32[]{:S(2)}, u32[]{:S(2)}) collective-permute-start(bf16[4,64,512]{2,1,0:T(8,128)(2,1)S(1)} %collective-permute-done.1), channel_id=1, source_target_pairs={{0,8},{8,16},{16,24},{24,0},{1,9},{9,17},{17,25},{25,1},{2,10},{10... | collective-permute-start | bytes 786440 | tf_op jit(solution)/shard_map/ppermute | solution.py:20
  170.1 22.7 %copy-start.1 = (s32[4,8]{1,0:T(4,128)S(1)}, s32[4,8]{1,0:T(4,128)}, u32[]{:S(2)}) copy-start(s32[4,8]{1,0:T(4,128)} %param.7) | copy-start | bytes 388
  170.2 23.2 %copy-start.2 = (f32[4,8]{1,0:T(4,128)S(1)}, f32[4,8]{1,0:T(4,128)}, u32[]{:S(2)}) copy-start(f32[4,8]{1,0:T(4,128)} %param.8) | copy-start | bytes 388
  189.2 26.5 %all-to-all-start.2 = ((bf16[4,1,8,2,7168]{4,3,0,1,2:T(2,128)(2,1)}), bf16[4,1,8,2,7168]{4,3,0,1,2:T(2,128)(2,1)S(1)}, u32[]{:S(2)}, u32[]{:S(2)}) async-start(bf16[4,1,8,2,7168]{4,3,0,1,2:T(2,128)(2,1)} %reshape.55), calls=%async_computation.2 | async-start | bytes 1835008 | tf_op jit(solution)/shard_map/all_to_all | solution.py:81
